TPU v7x, 512 devices: a whole 4x8x8 slice. The times are simulated.
512 devices in a mesh: lev: 8 (over x, z_lo), tile: 64 (over y, z_hi, core).
Axes of the slice: x: 4, y: 8, z: 8 (z_hi: 4, z_lo: 2; z = z_hi * 2 + z_lo), core: 2. Of those that a mesh axis runs over, the one named last changes fastest.
Arguments:
- thermal_deviation: float32 [64, 512, 4320], P('lev', 'tile'), may hold values from -6 to 6
- terrain_flag: int32 [512, 4320], P('tile'), may hold values 0 or 1
- frequency_share_limit_pointer: int32 [14], replicated, may hold values from 0 to 15
Outputs:
- coefficients: float32 [64, 512, 4320], P(None, 'tile', 'lev')
All inputs are finite; a program needn't handle non-finite values. No bound on the sum of `terrain_flag` on one device may be relied on, other than what follows from the above.
Results may differ from a plain program's by a relative error of at most 0.0003.
Values sent between devices are 32-bit elements; how exact they have to be, the bound alone decides.
A program may use at most 64 MiB of HBM per device.

v0:
```python
import functools
import math

import jax
import jax.numpy as jnp
from jax import lax
from jax.experimental import pallas as pl
from jax.experimental.pallas import tpu as pltpu
from jax.sharding import PartitionSpec as P

ALPHA = -1.586134342
BETA = -0.05298011854
GAMMA = 0.8829110762
DELTA = 0.4435068522
KAPPA = 1.149604398

LANES = 128
ROWS = 8
WIDTH = 4320
PARTS = 8
BLOCK = WIDTH // PARTS
FULL = BLOCK // LANES
TAIL = BLOCK - FULL * LANES
SPAN = FULL + 1
PADDED = 36
MESH = pl.DeviceIdType.MESH


def row_messages(even, odd):
    first = odd[0] + ALPHA * (even[0] + even[1])
    before = odd[-2] + ALPHA * (even[-2] + even[-1])
    p = odd[-1] + ALPHA * even[-1]
    q = p + GAMMA * (even[-1] + BETA * (before + p))
    return (p, q), (even[0], first)


def row_lift(even, odd, p, q, r, s):
    n = len(even)
    odd_one = [p + ALPHA * even[0]]
    odd_one += [odd[j] + ALPHA * (even[j] + (even[j + 1] if j + 1 < n else r)) for j in range(n)]
    even_two = [even[j] + BETA * (odd_one[j] + odd_one[j + 1]) for j in range(n)]
    even_two.append(r + BETA * (odd_one[n] + s))
    odd_three = [q + (ALPHA * (1.0 + GAMMA * BETA)) * even[0] + GAMMA * even_two[0]]
    odd_three += [odd_one[j + 1] + GAMMA * (even_two[j] + even_two[j + 1]) for j in range(n)]
    even_four = [even_two[j] + DELTA * (odd_three[j] + odd_three[j + 1]) for j in range(n)]
    return even_four, odd_three[1:]


def turn(value, amount):
    return pltpu.roll(value, amount % LANES, axis=1)


def column_lift(even, odd, step, lane):
    n = len(even)

    def following(tiles):
        rolled = [turn(v, -step) for v in tiles]
        return [jnp.where(lane >= LANES - step, rolled[(j + 1) % n], rolled[j]) for j in range(n)]

    def preceding(tiles):
        rolled = [turn(v, step) for v in tiles]
        return [jnp.where(lane < step, rolled[j - 1], rolled[j]) for j in range(n)]

    odd = [o + ALPHA * (e + f) for o, e, f in zip(odd, even, following(even))]
    even = [e + BETA * (o + f) for e, o, f in zip(even, odd, preceding(odd))]
    odd = [o + GAMMA * (e + f) for o, e, f in zip(odd, even, following(even))]
    even = [e + DELTA * (o + f) for e, o, f in zip(even, odd, preceding(odd))]
    return even, odd


def split_pair(a, b, step, keep):
    even = [jnp.where(keep, u, turn(v, step)) for u, v in zip(a, b)]
    odd = [jnp.where(keep, turn(u, -step), v) for u, v in zip(a, b)]
    return even, odd


def join_pair(even, odd, step, keep):
    a = [jnp.where(keep, e, turn(o, step)) for e, o in zip(even, odd)]
    b = [jnp.where(keep, turn(e, -step), o) for e, o in zip(even, odd)]
    return a, b


def tap_values():
    root = math.sqrt(3.0)
    scale = 4.0 * math.sqrt(2.0)
    low = [(1.0 + root) / scale, (3.0 + root) / scale, (3.0 - root) / scale, (1.0 - root) / scale]
    return low, [low[3], -low[2], low[1], -low[0]]


def cutoff_pattern(pointer_ref, half):
    row = lax.broadcasted_iota(jnp.int32, (ROWS, LANES), 0)
    col = lax.broadcasted_iota(jnp.int32, (ROWS, LANES), 1)
    fine = 3 + 2 * (row % 2) + col % 2
    coarse = 2 * (row // 2 % 2) + col // 2 % 2
    band = jnp.where(row % 2 + col % 2 > 0, fine, coarse)
    power = jnp.zeros((ROWS, LANES), jnp.int32)
    for number in range(7):
        power = jnp.where(band == number, pointer_ref[7 * half + number], power)
    cutoff = jnp.full((ROWS, LANES), 0.05, jnp.float32)
    for bit in range(4):
        factor = 1.25 ** (2**bit)
        cutoff = jnp.where((power // 2**bit) % 2 == 1, cutoff * factor, cutoff)
    return cutoff


def kernel(
    tiles_count,
    x_ref,
    flag_ref,
    pointer_ref,
    out_ref,
    field,
    to_next,
    to_prev,
    from_prev,
    from_next,
    window,
    hold,
    to_next2,
    to_prev2,
    from_prev2,
    from_next2,
    send_main,
    send_tail,
    recv_main,
    recv_tail,
    levels,
    edge_send,
    edge_recv,
    edge2_send,
    edge2_recv,
    main_send,
    main_recv,
    tail_send,
    tail_recv,
    own_sem,
):
    me = lax.axis_index("lev")
    row_block = lax.axis_index("tile")
    has_prev = row_block > 0
    has_next = row_block < tiles_count - 1
    lane = lax.broadcasted_iota(jnp.int32, (ROWS, LANES), 1)
    lane_even = lane % 2 == 0
    lane_low = lane % 4 < 2
    nothing = jnp.zeros((ROWS, LANES), jnp.float32)

    barrier = pltpu.get_barrier_semaphore()
    for step in range(1, PARTS):
        pl.semaphore_signal(
            barrier,
            inc=1,
            device_id={"lev": lax.rem(me + step, PARTS)},
            device_id_type=MESH,
        )

    @pl.when(has_prev)
    def _():
        pl.semaphore_signal(
            barrier, inc=1, device_id={"tile": row_block - 1}, device_id_type=MESH
        )

    @pl.when(has_next)
    def _():
        pl.semaphore_signal(
            barrier, inc=1, device_id={"tile": row_block + 1}, device_id_type=MESH
        )

    field[pl.ds(0, ROWS * ROWS), :] = jnp.zeros((ROWS * ROWS, LANES), jnp.float32)
    field[pl.ds((PADDED - 2) * ROWS * ROWS, 2 * ROWS * ROWS), :] = jnp.zeros(
        (2 * ROWS * ROWS, LANES), jnp.float32
    )
    last = WIDTH // LANES
    rest = WIDTH - last * LANES

    def load_tile(tile, _):
        columns = pl.ds(pl.multiple_of(tile * LANES, LANES), LANES)
        water = (1 - flag_ref[:, columns]).astype(jnp.float32)
        for level in range(ROWS):
            start = pl.multiple_of((tile + 1) * ROWS * ROWS + level * ROWS, ROWS)
            field[pl.ds(start, ROWS), :] = x_ref[level, :, columns] * water
        return 0

    lax.fori_loop(0, last, load_tile, 0)
    water = (1 - flag_ref[:, pl.ds(last * LANES, rest)]).astype(jnp.float32)
    for level in range(ROWS):
        start = (last + 1) * ROWS * ROWS + level * ROWS
        field[pl.ds(start, ROWS), pl.ds(0, rest)] = (
            x_ref[level, :, pl.ds(last * LANES, rest)] * water
        )

    def rows_of(tile):
        return [
            field[pl.ds(tile * ROWS * ROWS + row, ROWS, stride=ROWS), :] for row in range(ROWS)
        ]

    def edge_tile(tile, _):
        rows = rows_of(tile)
        forward, backward = row_messages(rows[0::2], rows[1::2])
        for i in range(2):
            to_next[tile, i] = forward[i]
            to_prev[tile, i] = backward[i]
        return 0

    lax.fori_loop(1, PADDED - 1, edge_tile, 0)

    for ref in (from_prev, from_next):
        for tile in (0, PADDED - 1):
            for i in range(2):
                ref[tile, i] = nothing

    def clear(edge, edge2):
        def clear_tile(tile, _):
            for i in range(2):
                edge[tile, i] = nothing
            return 0

        def clear_second(k, _):
            for j in range(SPAN):
                edge2[k, j] = nothing
            return 0

        lax.fori_loop(1, PADDED - 1, clear_tile, 0)
        lax.fori_loop(0, PARTS, clear_second, 0)

    @pl.when(jnp.logical_not(has_prev))
    def _():
        clear(from_prev, from_prev2)

    @pl.when(jnp.logical_not(has_next))
    def _():
        clear(from_next, from_next2)

    pl.semaphore_wait(
        barrier, PARTS - 1 + jnp.where(has_prev, 1, 0) + jnp.where(has_next, 1, 0)
    )

    body = pl.ds(1, PADDED - 2)

    def edge_forward():
        return pltpu.make_async_remote_copy(
            src_ref=to_next.at[body],
            dst_ref=from_prev.at[body],
            send_sem=edge_send.at[0],
            recv_sem=edge_recv.at[0],
            device_id={"tile": row_block + 1},
            device_id_type=MESH,
        )

    def edge_backward():
        return pltpu.make_async_remote_copy(
            src_ref=to_prev.at[body],
            dst_ref=from_next.at[body],
            send_sem=edge_send.at[1],
            recv_sem=edge_recv.at[1],
            device_id={"tile": row_block - 1},
            device_id_type=MESH,
        )

    def edge2_forward(k):
        return pltpu.make_async_remote_copy(
            src_ref=to_next2.at[k],
            dst_ref=from_prev2.at[k],
            send_sem=edge2_send.at[0, k],
            recv_sem=edge2_recv.at[0, k],
            device_id={"tile": row_block + 1},
            device_id_type=MESH,
        )

    def edge2_backward(k):
        return pltpu.make_async_remote_copy(
            src_ref=to_prev2.at[k],
            dst_ref=from_next2.at[k],
            send_sem=edge2_send.at[1, k],
            recv_sem=edge2_recv.at[1, k],
            device_id={"tile": row_block - 1},
            device_id_type=MESH,
        )

    def target(k):
        return lax.rem(me + 1 + k, PARTS)

    def main_copy(k, parity):
        return pltpu.make_async_remote_copy(
            src_ref=send_main.at[k, :, parity],
            dst_ref=recv_main.at[me, :, parity],
            send_sem=main_send.at[parity, k],
            recv_sem=main_recv.at[parity, k],
            device_id={"lev": target(k)},
            device_id_type=MESH,
        )

    def tail_copy(k):
        return pltpu.make_async_remote_copy(
            src_ref=send_tail.at[k],
            dst_ref=recv_tail.at[me],
            send_sem=tail_send.at[k],
            recv_sem=tail_recv.at[k],
            device_id={"lev": target(k)},
            device_id_type=MESH,
        )

    own = PARTS - 1

    def own_main(parity):
        return pltpu.make_async_copy(
            send_main.at[own, :, parity], recv_main.at[me, :, parity], own_sem.at[parity]
        )

    def own_tail():
        return pltpu.make_async_copy(send_tail.at[own], recv_tail.at[me], own_sem.at[2])

    @pl.when(has_next)
    def _():
        edge_forward().start()

    @pl.when(has_prev)
    def _():
        edge_backward().start()

    @pl.when(has_prev)
    def _():
        edge_forward().wait_recv()

    @pl.when(has_next)
    def _():
        edge_backward().wait_recv()

    def put_rows(k, parity, rows):
        tail = rows[0][FULL]
        for i in range(4):
            for j in range(FULL):
                send_main[k, i, parity, pl.ds(j * ROWS, ROWS), :] = rows[i][j]
            if i > 0:
                tail = jnp.where(lane >= i * TAIL, turn(rows[i][FULL], i * TAIL), tail)
        send_tail[k, parity] = tail

    def first_stage(k, _):
        block = target(k)
        first = (block * BLOCK) // LANES
        shift = block * BLOCK - first * LANES
        back = lax.rem(LANES - shift, LANES)
        inside = lane < LANES - shift
        for i in range(SPAN + 2):
            rows = rows_of(first + i)
            even, odd = row_lift(
                rows[0::2],
                rows[1::2],
                from_prev[first + i, 0],
                from_prev[first + i, 1],
                from_next[first + i, 0],
                from_next[first + i, 1],
            )
            for j in range(4):
                window[2 * j, i] = pltpu.roll(even[j], back, axis=1)
                window[2 * j + 1, i] = pltpu.roll(odd[j], back, axis=1)

        def aligned(row):
            tiles = [window[row, i] for i in range(SPAN + 2)]
            moved = [jnp.where(inside, tiles[i], tiles[i + 1]) for i in range(SPAN + 1)]
            return moved[1:SPAN] + [jnp.where(lane < LANES // 2, moved[SPAN], moved[0])]

        def lifted(a, b):
            even, odd = split_pair(aligned(a), aligned(b), 1, lane_even)
            return column_lift(even, odd, 1 * 2, lane)

        rows = [None] * ROWS
        for a, b in ((1, 5), (3, 7)):
            even, odd = lifted(a, b)
            odd = [v * (KAPPA * KAPPA) for v in odd]
            rows[a], rows[b] = join_pair(even, odd, 1, lane_even)
        put_rows(k, 1, rows[1::2])

        @pl.when(k < own)
        def _():
            main_copy(k, 1).start()

        @pl.when(k == own)
        def _():
            own_main(1).start()

        within = jnp.logical_or(
            lane < TAIL,
            jnp.logical_or(
                jnp.logical_and(lane < LANES // 2, block < PARTS - 1),
                jnp.logical_and(lane >= LANES // 2, block > 0),
            ),
        )
        low_a, high_a = lifted(0, 4)
        low_b, high_b = lifted(2, 6)
        low_a[FULL] = jnp.where(within, low_a[FULL], 0.0)
        low_b[FULL] = jnp.where(within, low_b[FULL], 0.0)
        even, odd = split_pair(low_a, low_b, 2, lane_low)
        even, odd = column_lift(even, odd, 4, lane)
        low_a, low_b = join_pair(even, odd, 2, lane_low)
        c0, c2 = join_pair(low_a, high_a, 1, lane_even)
        c1, c3 = join_pair(low_b, high_b, 1, lane_even)
        for j in range(SPAN):
            for i, row in enumerate((c0, c1, c2, c3)):
                hold[k, i, j] = row[j]
            (p, q), (r, s) = row_messages([c0[j], c2[j]], [c1[j], c3[j]])
            to_next2[k, j] = jnp.where(lane_even, p, turn(q, 1))
            to_prev2[k, j] = jnp.where(lane_even, r, turn(s, 1))

        @pl.when(has_next)
        def _():
            edge2_forward(k).start()

        @pl.when(has_prev)
        def _():
            edge2_backward(k).start()

        return 0

    lax.fori_loop(0, PARTS, first_stage, 0)

    square = KAPPA * KAPPA
    one = jnp.ones((ROWS, LANES), jnp.float32)
    scale_even = jnp.where(
        lane_even, jnp.where(lane_low, 1.0 / (square * square), 1.0 / square), one
    )
    scale_odd = jnp.where(jnp.logical_and(lane_even, lane_low), 1.0 / square, one)

    def second_stage(k, _):
        @pl.when(has_prev)
        def _():
            edge2_forward(k).wait_recv()

        @pl.when(has_next)
        def _():
            edge2_backward(k).wait_recv()

        rows = [[None] * SPAN for _ in range(4)]
        for j in range(SPAN):
            c = [hold[k, i, j] for i in range(4)]
            p = from_prev2[k, j]
            r = from_next2[k, j]
            even, odd = row_lift(c[0::2], c[1::2], p, turn(p, -1), r, turn(r, -1))
            for i in range(2):
                rows[2 * i][j] = jnp.where(lane_even, even[i], c[2 * i]) * scale_even
                rows[2 * i + 1][j] = jnp.where(lane_even, odd[i], c[2 * i + 1]) * scale_odd
        put_rows(k, 0, rows)

        @pl.when(k < own)
        def _():
            main_copy(k, 0).start()
            tail_copy(k).start()

        @pl.when(k == own)
        def _():
            own_main(0).start()
            own_tail().start()

        return 0

    lax.fori_loop(0, PARTS, second_stage, 0)

    own_main(1).wait()
    own_main(0).wait()
    own_tail().wait()

    def arrived(k, _):
        main_copy(k, 1).wait_recv()
        main_copy(k, 0).wait_recv()
        tail_copy(k).wait_recv()
        return 0

    lax.fori_loop(0, own, arrived, 0)

    def spread(source, _):
        for parity in range(2):
            tail = recv_tail[source, parity]
            for i in range(4):
                start = ((source * ROWS + 2 * i + parity) * SPAN) * ROWS
                for j in range(FULL):
                    levels[pl.ds(pl.multiple_of(start + j * ROWS, ROWS), ROWS), :] = recv_main[
                        source, i, parity, pl.ds(j * ROWS, ROWS), :
                    ]
                levels[pl.ds(pl.multiple_of(start + FULL * ROWS, ROWS), ROWS), :] = turn(
                    tail, -i * TAIL
                )
        return 0

    lax.fori_loop(0, PARTS, spread, 0)

    low_taps, high_taps = tap_values()
    cutoffs = [cutoff_pattern(pointer_ref, half) for half in range(2)]

    def level_tile(source, level, j):
        start = source * ROWS * SPAN * ROWS + j * ROWS + level
        return levels[pl.ds(start, ROWS, stride=SPAN * ROWS), :]

    def vertical(source, _):
        after = lax.rem(source + 1, PARTS)
        for j in range(SPAN):
            taken = [level_tile(source, level, j) for level in range(ROWS)]
            taken += [level_tile(after, level, j) for level in range(2)]
            for i in range(ROWS // 2):
                for half, taps in enumerate((low_taps, high_taps)):
                    value = taps[0] * taken[2 * i]
                    for tap in range(1, 4):
                        value = value + taps[tap] * taken[2 * i + tap]
                    cutoff = cutoffs[half]
                    value = value - jnp.minimum(jnp.maximum(value, -cutoff), cutoff)
                    row = half * PARTS * ROWS // 2 + source * (ROWS // 2) + i
                    if j == FULL:
                        out_ref[row, :, pl.ds(FULL * LANES, TAIL)] = value[:, :TAIL]
                    else:
                        out_ref[row, :, pl.ds(j * LANES, LANES)] = value
        return 0

    lax.fori_loop(0, PARTS, vertical, 0)

    @pl.when(has_next)
    def _():
        edge_forward().wait_send()

    @pl.when(has_prev)
    def _():
        edge_backward().wait_send()

    def sent(k, _):
        @pl.when(has_next)
        def _():
            edge2_forward(k).wait_send()

        @pl.when(has_prev)
        def _():
            edge2_backward(k).wait_send()

        @pl.when(k < own)
        def _():
            main_copy(k, 1).wait_send()
            main_copy(k, 0).wait_send()
            tail_copy(k).wait_send()

        return 0

    lax.fori_loop(0, PARTS, sent, 0)


def local(tiles_count, thermal_deviation, terrain_flag, frequency_share_limit_pointer):
    tile = (ROWS, LANES)
    vmem = lambda *shape: pltpu.VMEM(shape, jnp.float32)
    dma = pltpu.SemaphoreType.DMA
    return pl.pallas_call(
        functools.partial(kernel, tiles_count),
        out_shape=jax.ShapeDtypeStruct((PARTS * ROWS, ROWS, BLOCK), jnp.float32),
        in_specs=[
            pl.BlockSpec(memory_space=pltpu.VMEM),
            pl.BlockSpec(memory_space=pltpu.VMEM),
            pl.BlockSpec(memory_space=pltpu.SMEM),
        ],
        out_specs=pl.BlockSpec(memory_space=pltpu.VMEM),
        scratch_shapes=[
            vmem(PADDED * ROWS * ROWS, LANES),
            vmem(PADDED, 2, *tile),
            vmem(PADDED, 2, *tile),
            vmem(PADDED, 2, *tile),
            vmem(PADDED, 2, *tile),
            vmem(ROWS, SPAN + 2, *tile),
            vmem(PARTS, 4, SPAN, *tile),
            vmem(PARTS, SPAN, *tile),
            vmem(PARTS, SPAN, *tile),
            vmem(PARTS, SPAN, *tile),
            vmem(PARTS, SPAN, *tile),
            vmem(PARTS, 4, 2, FULL * ROWS, LANES),
            vmem(PARTS, 2, *tile),
            vmem(PARTS, 4, 2, FULL * ROWS, LANES),
            vmem(PARTS, 2, *tile),
            vmem(PARTS * ROWS * SPAN * ROWS, LANES),
            dma((2,)),
            dma((2,)),
            dma((2, PARTS)),
            dma((2, PARTS)),
            dma((2, PARTS)),
            dma((2, PARTS)),
            dma((PARTS,)),
            dma((PARTS,)),
            dma((3,)),
        ],
        compiler_params=pltpu.CompilerParams(
            collective_id=0, has_side_effects=True, vmem_limit_bytes=32 * 1024 * 1024
        ),
    )(thermal_deviation, terrain_flag, frequency_share_limit_pointer)


def solution(mesh):
    placed = (P("lev", "tile", None), P("tile", None), P())
    return jax.shard_map(
        functools.partial(local, mesh.shape["tile"]),
        mesh=mesh,
        in_specs=placed,
        out_specs=P(None, "tile", "lev"),
        check_vma=False,
    )
```

profile of v0, /device:TPU:81, one launch (start us, length us, event | category | flops | bytes accessed | tf_op | source)
XLA Modules:
  0.0 46.6 jit_solution(973190776387781738)
XLA Ops:
  0.0 0.0 copy-start
  0.0 1.2 %copy-done = f32[8,8,4320]{2,1,0:T(8,128)S(1)} copy-done((f32[8,8,4320]{2,1,0:T(8,128)S(1)}, f32[8,8,4320]{2,1,0:T(8,128)}, u32[]{:S(2)}) %copy-start) | copy-done | bytes 1105944
  1.2 0.0 copy-start.1
  1.3 0.9 %copy-done.1 = s32[8,4320]{1,0:T(8,128)S(1)} copy-done((s32[8,4320]{1,0:T(8,128)S(1)}, s32[8,4320]{1,0:T(8,128)}, u32[]{:S(2)}) %copy-start.1) | copy-done | bytes 138264
  2.2 0.0 copy-start.2
  2.2 0.7 %copy-done.2 = s32[14]{0:T(128)S(1)} copy-done((s32[14]{0:T(128)S(1)}, s32[14]{0:T(128)}, u32[]{:S(2)}) %copy-start.2) | copy-done | bytes 80
  2.8 42.7 %shard_map.37 = f32[64,8,540]{2,1,0:T(8,128)S(1)} custom-call(f32[8,8,4320]{2,1,0:T(8,128)S(1)} %copy-done, s32[8,4320]{1,0:T(8,128)S(1)} %copy-done.1, s32[14]{0:T(128)S(1)} %copy-done.2), custom_call_target="tpu_custom_call" | custom-call | tf_op jit(solution)/shard_map/pallas_call | solution.py:545
  45.5 1.1 %copy.5 = f32[64,8,540]{2,1,0:T(8,128)} copy(f32[64,8,540]{2,1,0:T(8,128)S(1)} %shard_map.37) | data formatting | bytes 2211840
Async XLA Ops:
  0.0 1.2 %copy-start = (f32[8,8,4320]{2,1,0:T(8,128)S(1)}, f32[8,8,4320]{2,1,0:T(8,128)}, u32[]{:S(2)}) copy-start(f32[8,8,4320]{2,1,0:T(8,128)} %x_ref.1) | copy-start | bytes 3317764
  1.2 0.9 %copy-start.1 = (s32[8,4320]{1,0:T(8,128)S(1)}, s32[8,4320]{1,0:T(8,128)}, u32[]{:S(2)}) copy-start(s32[8,4320]{1,0:T(8,128)} %flag_ref.1) | copy-start | bytes 414724
  2.2 0.7 %copy-start.2 = (s32[14]{0:T(128)S(1)}, s32[14]{0:T(128)}, u32[]{:S(2)}) copy-start(s32[14]{0:T(128)} %pointer_ref.1) | copy-start | bytes 172
where the time goes:
time: 46.8 us; the launch traced here: 46.6 us
  Pallas kernels  42.7 us (91%)
  local copies, waits for them, and re-layouts  3.87 us (8%)
    pallas_call x1, Pallas kernels, local(): pl.pallas_call(functools.partial(kernel, tiles_count), out_shape=jax.Shap...  42.7 us
    unnamed x7, local copies, waits for them, and re-layouts  3.87 us

commit v1 on v0

v1 whole, which is shorter than its diff:
```python
import functools
import math

import jax
import jax.numpy as jnp
import numpy as np
from jax import lax
from jax.experimental import pallas as pl
from jax.experimental.pallas import tpu as pltpu
from jax.sharding import PartitionSpec as P

ALPHA = -1.586134342
BETA = -0.05298011854
GAMMA = 0.8829110762
DELTA = 0.4435068522
KAPPA = 1.149604398

LANES = 128
ROWS = 8
WIDTH = 4320
PARTS = 8
BLOCK = WIDTH // PARTS
FULL = BLOCK // LANES
TAIL = BLOCK - FULL * LANES
SPAN = FULL + 1
WINDOWS = 4
WIDE = 9
LAST = 2 * BLOCK - (WIDE - 1) * LANES
HALO = (LANES - LAST) // 2
PADDED = 36
GROUP = ROWS * ROWS
ROW_LINES = FULL * ROWS
SLOTS = (3, 5, 7, 1, 0, 2, 4, 6)
ROW_AT = {row: i * ROW_LINES for i, row in enumerate(SLOTS)}
ODD_TAILS = ROWS * ROW_LINES
EVEN_TAILS = ODD_TAILS + ROWS
MESSAGE = EVEN_TAILS + ROWS
PIECES = (
    (0, ROW_LINES),
    (ROW_LINES, 2 * ROW_LINES),
    (3 * ROW_LINES, ROW_LINES),
    (4 * ROW_LINES, MESSAGE - 4 * ROW_LINES),
)
TAIL_AT = {row: row // 2 for row in range(ROWS)}
CHAIN = 8
MESH = pl.DeviceIdType.MESH


def impulse_responses():
    low, high = [], []
    for distance in range(5):
        for centre, taps in ((16, low), (17, high)):
            signal = np.zeros(34)
            signal[centre + distance] = 1.0
            even, odd = signal[0::2].copy(), signal[1::2].copy()
            odd[:-1] += ALPHA * (even[:-1] + even[1:])
            even[1:] += BETA * (odd[:-1] + odd[1:])
            odd[:-1] += GAMMA * (even[:-1] + even[1:])
            even[1:] += DELTA * (odd[:-1] + odd[1:])
            taps.append(float(even[8] if centre == 16 else odd[8]))
    return low, high[:4]


LOW, HIGH = impulse_responses()


def row_messages(even, odd):
    first = odd[0] + ALPHA * (even[0] + even[1])
    before = odd[-2] + ALPHA * (even[-2] + even[-1])
    p = odd[-1] + ALPHA * even[-1]
    q = p + GAMMA * (even[-1] + BETA * (before + p))
    return (p, q), (even[0], first)


def row_lift(even, odd, p, q, r, s):
    n = len(even)
    odd_one = [p + ALPHA * even[0]]
    odd_one += [odd[j] + ALPHA * (even[j] + (even[j + 1] if j + 1 < n else r)) for j in range(n)]
    even_two = [even[j] + BETA * (odd_one[j] + odd_one[j + 1]) for j in range(n)]
    even_two.append(r + BETA * (odd_one[n] + s))
    odd_three = [q + (ALPHA * (1.0 + GAMMA * BETA)) * even[0] + GAMMA * even_two[0]]
    odd_three += [odd_one[j + 1] + GAMMA * (even_two[j] + even_two[j + 1]) for j in range(n)]
    even_four = [even_two[j] + DELTA * (odd_three[j] + odd_three[j + 1]) for j in range(n)]
    return even_four, odd_three[1:]


def turn(value, amount):
    return pltpu.roll(value, amount % LANES, axis=1)


def column_lift(even, odd, step, lane, high_scale=1.0):
    n = len(even)

    def moved(tiles, distance):
        lanes = distance * step
        rolled = [turn(v, -lanes) for v in tiles]
        if distance > 0:
            return [jnp.where(lane >= LANES - lanes, rolled[(j + 1) % n], rolled[j]) for j in range(n)]
        return [jnp.where(lane < -lanes, rolled[j - 1], rolled[j]) for j in range(n)]

    even_at = {d: moved(even, d) for d in (-2, -1, 1, 2)}
    odd_at = {d: moved(odd, d) for d in (-2, -1, 1)}
    high_taps = [high_scale * tap for tap in HIGH]
    low, high = [], []
    for j in range(n):
        low.append(
            LOW[0] * even[j]
            + LOW[1] * (odd_at[-1][j] + odd[j])
            + LOW[2] * (even_at[-1][j] + even_at[1][j])
            + LOW[3] * (odd_at[-2][j] + odd_at[1][j])
            + LOW[4] * (even_at[-2][j] + even_at[2][j])
        )
        high.append(
            high_taps[0] * odd[j]
            + high_taps[1] * (even[j] + even_at[1][j])
            + high_taps[2] * (odd_at[-1][j] + odd_at[1][j])
            + high_taps[3] * (even_at[-1][j] + even_at[2][j])
        )
    return low, high


def split_pair(a, b, step, keep):
    even = [jnp.where(keep, u, turn(v, step)) for u, v in zip(a, b)]
    odd = [jnp.where(keep, turn(u, -step), v) for u, v in zip(a, b)]
    return even, odd


def join_pair(even, odd, step, keep):
    a = [jnp.where(keep, e, turn(o, step)) for e, o in zip(even, odd)]
    b = [jnp.where(keep, turn(e, -step), o) for e, o in zip(even, odd)]
    return a, b


def tap_values():
    root = math.sqrt(3.0)
    scale = 4.0 * math.sqrt(2.0)
    low = [(1.0 + root) / scale, (3.0 + root) / scale, (3.0 - root) / scale, (1.0 - root) / scale]
    return low, [low[3], -low[2], low[1], -low[0]]


def cutoff_pattern(pointer_ref, half):
    row = lax.broadcasted_iota(jnp.int32, (ROWS, LANES), 0)
    col = lax.broadcasted_iota(jnp.int32, (ROWS, LANES), 1)
    fine = 3 + 2 * (row % 2) + col % 2
    coarse = 2 * (row // 2 % 2) + col // 2 % 2
    band = jnp.where(row % 2 + col % 2 > 0, fine, coarse)
    power = jnp.zeros((ROWS, LANES), jnp.int32)
    for number in range(7):
        power = jnp.where(band == number, pointer_ref[7 * half + number], power)
    cutoff = jnp.full((ROWS, LANES), 0.05, jnp.float32)
    for bit in range(4):
        factor = 1.25 ** (2**bit)
        cutoff = jnp.where((power // 2**bit) % 2 == 1, cutoff * factor, cutoff)
    return cutoff


def kernel(
    tiles_count,
    x_hbm,
    flag_hbm,
    pointer_ref,
    out_hbm,
    out_ref,
    x_ref,
    flag_ref,
    field,
    aligned,
    to_next,
    to_prev,
    from_prev,
    from_next,
    window,
    hold,
    to_next2,
    to_prev2,
    from_prev2,
    from_next2,
    send,
    recv,
    levels,
    load_sem,
    edge_send,
    edge_recv,
    edge2_send,
    edge2_recv,
    block_send,
    block_recv,
    own_sem,
    store_sem,
    ready,
):
    me = lax.axis_index("lev")
    row_block = lax.axis_index("tile")
    place, half = me // 2, lax.rem(me, 2)
    has_prev = row_block > 0
    has_next = row_block < tiles_count - 1
    seam_prev = lax.rem(row_block, CHAIN) == 0
    seam_next = lax.rem(row_block, CHAIN) == CHAIN - 1
    early_prev = jnp.logical_and(has_prev, jnp.logical_not(seam_prev))
    late_prev = jnp.logical_and(has_prev, seam_prev)
    early_next = jnp.logical_and(has_next, seam_next)
    late_next = jnp.logical_and(has_next, jnp.logical_not(seam_next))
    row_1_first = lax.rem(row_block, CHAIN) == 1
    lane = lax.broadcasted_iota(jnp.int32, (ROWS, LANES), 1)
    lane_even = lane % 2 == 0
    lane_low = lane % 4 < 2
    nothing = jnp.zeros((ROWS, LANES), jnp.float32)

    barrier = pltpu.get_barrier_semaphore()
    for step in range(1, PARTS):
        pl.semaphore_signal(
            barrier,
            inc=1,
            device_id={"lev": lax.rem(me + step, PARTS)},
            device_id_type=MESH,
        )

    @pl.when(late_prev)
    def _():
        pl.semaphore_signal(
            barrier, inc=1, device_id={"tile": row_block - 1}, device_id_type=MESH
        )

    @pl.when(late_next)
    def _():
        pl.semaphore_signal(
            barrier, inc=1, device_id={"tile": row_block + 1}, device_id_type=MESH
        )

    loads = [
        pltpu.make_async_copy(x_hbm.at[level], x_ref.at[level], load_sem.at[level])
        for level in range(ROWS)
    ]
    loads.append(pltpu.make_async_copy(flag_hbm, flag_ref, load_sem.at[ROWS]))
    for load in loads:
        load.start()

    def clear(edge, edge2):
        def clear_window(k, _):
            for j in range(WIDE):
                edge[k, j, 0] = nothing
                edge[k, j, 1] = nothing
                edge2[k, j] = nothing
            return 0

        lax.fori_loop(0, WINDOWS, clear_window, 0)

    @pl.when(jnp.logical_not(has_prev))
    def _():
        clear(from_prev, from_prev2)

    @pl.when(jnp.logical_not(has_next))
    def _():
        clear(from_next, from_next2)

    field[pl.ds(0, GROUP), :] = jnp.zeros((GROUP, LANES), jnp.float32)
    field[pl.ds((PADDED - 2) * GROUP, 2 * GROUP), :] = jnp.zeros((2 * GROUP, LANES), jnp.float32)
    pl.semaphore_wait(
        barrier, PARTS - 1 + jnp.where(early_prev, 1, 0) + jnp.where(early_next, 1, 0)
    )

    @pl.when(early_prev)
    def _():
        pl.semaphore_signal(
            ready.at[0], inc=1, device_id={"tile": row_block - 1}, device_id_type=MESH
        )

    @pl.when(early_next)
    def _():
        pl.semaphore_signal(
            ready.at[1], inc=1, device_id={"tile": row_block + 1}, device_id_type=MESH
        )

    for load in loads:
        load.wait()

    whole = WIDTH // LANES
    rest = WIDTH - whole * LANES

    def load_tile(tile, _):
        columns = pl.ds(pl.multiple_of(tile * LANES, LANES), LANES)
        water = (1 - flag_ref[:, columns]).astype(jnp.float32)
        for level in range(ROWS):
            start = pl.multiple_of((tile + 1) * GROUP + level * ROWS, ROWS)
            field[pl.ds(start, ROWS), :] = x_ref[level, :, columns] * water
        return 0

    lax.fori_loop(0, whole, load_tile, 0)
    water = (1 - flag_ref[:, pl.ds(whole * LANES, rest)]).astype(jnp.float32)
    for level in range(ROWS):
        start = (whole + 1) * GROUP + level * ROWS
        field[pl.ds(start, ROWS), pl.ds(0, rest)] = (
            x_ref[level, :, pl.ds(whole * LANES, rest)] * water
        )

    def window_of(k):
        return lax.rem(place + 1 + k, WINDOWS)

    def edge_forward(k):
        return pltpu.make_async_remote_copy(
            src_ref=to_next.at[k],
            dst_ref=from_prev.at[k],
            send_sem=edge_send.at[0, k],
            recv_sem=edge_recv.at[0, k],
            device_id={"tile": row_block + 1},
            device_id_type=MESH,
        )

    def edge_backward(k):
        return pltpu.make_async_remote_copy(
            src_ref=to_prev.at[k],
            dst_ref=from_next.at[k],
            send_sem=edge_send.at[1, k],
            recv_sem=edge_recv.at[1, k],
            device_id={"tile": row_block - 1},
            device_id_type=MESH,
        )

    def edge2_forward(k):
        return pltpu.make_async_remote_copy(
            src_ref=to_next2.at[k],
            dst_ref=from_prev2.at[k],
            send_sem=edge2_send.at[0, k],
            recv_sem=edge2_recv.at[0, k],
            device_id={"tile": row_block + 1},
            device_id_type=MESH,
        )

    def edge2_backward(k):
        return pltpu.make_async_remote_copy(
            src_ref=to_prev2.at[k],
            dst_ref=from_next2.at[k],
            send_sem=edge2_send.at[1, k],
            recv_sem=edge2_recv.at[1, k],
            device_id={"tile": row_block - 1},
            device_id_type=MESH,
        )

    def block_copy(k, b, piece):
        lines = pl.ds(*PIECES[piece])
        return pltpu.make_async_remote_copy(
            src_ref=send.at[2 * k + b, lines],
            dst_ref=recv.at[me, lines],
            send_sem=block_send.at[piece, 2 * k + b],
            recv_sem=block_recv.at[piece, me],
            device_id={"lev": 2 * window_of(k) + b},
            device_id_type=MESH,
        )

    def from_source(source, piece):
        lines = pl.ds(*PIECES[piece])
        return pltpu.make_async_remote_copy(
            src_ref=send.at[0, lines],
            dst_ref=recv.at[source, lines],
            send_sem=block_send.at[piece, 0],
            recv_sem=block_recv.at[piece, source],
            device_id={"lev": source},
            device_id_type=MESH,
        )

    def own_copy(piece):
        lines = pl.ds(*PIECES[piece])
        return pltpu.make_async_copy(
            send.at[2 * (WINDOWS - 1) + half, lines], recv.at[me, lines], own_sem.at[piece]
        )

    def start_blocks(k, piece):
        for b in range(2):
            is_own = jnp.logical_and(k == WINDOWS - 1, half == b)

            @pl.when(jnp.logical_not(is_own))
            def _():
                block_copy(k, b, piece).start()

            @pl.when(is_own)
            def _():
                own_copy(piece).start()

    def put_row(k, row, tiles, first=False):
        at = ROW_AT[row]
        for j in range(FULL):
            send[2 * k, pl.ds(at + j * ROWS, ROWS), :] = tiles[j]
        rolled = [turn(tiles[j], -TAIL) for j in range(FULL, WIDE)]
        for j in range(FULL):
            send[2 * k + 1, pl.ds(at + j * ROWS, ROWS), :] = jnp.where(
                lane < LANES - TAIL, rolled[j], rolled[j + 1]
            )
        start = TAIL * TAIL_AT[row]
        lines = pl.ds(ODD_TAILS if row % 2 else EVEN_TAILS, ROWS)
        for b, tail in enumerate((tiles[FULL], rolled[FULL])):
            tail = turn(tail, start)
            if not first:
                mine = jnp.logical_and(lane >= start, lane < start + TAIL)
                tail = jnp.where(mine, tail, send[2 * k + b, lines, :])
            send[2 * k + b, lines, :] = tail

    def rows_of(k, j):
        start = (k * WIDE + j) * GROUP
        return [aligned[pl.ds(start + row, ROWS, stride=ROWS), :] for row in range(ROWS)]

    def edge_stage(k, _):
        w = window_of(k)
        first = (w * 2 * BLOCK) // LANES
        shift = w * 2 * BLOCK - first * LANES
        back = lax.rem(LANES - shift, LANES)
        inside = lane < LANES - shift
        halo, before = None, None
        for i in range(WIDE + 2):
            tile = [
                pltpu.roll(
                    field[pl.ds(pl.multiple_of((first + i) * GROUP + level * ROWS, ROWS), ROWS), :],
                    back,
                    axis=1,
                )
                for level in range(ROWS)
            ]
            if i > 0:
                moved = [jnp.where(inside, u, v) for u, v in zip(before, tile)]
                if i == 1:
                    halo = moved
                else:
                    if i == WIDE + 1:
                        moved = [
                            jnp.where(lane < LAST + HALO, u, v) for u, v in zip(moved, halo)
                        ]
                    for level in range(ROWS):
                        start = (k * WIDE + i - 2) * GROUP + level * ROWS
                        aligned[pl.ds(pl.multiple_of(start, ROWS), ROWS), :] = moved[level]
            before = tile
        for j in range(WIDE):
            rows = rows_of(k, j)
            forward, backward = row_messages(rows[0::2], rows[1::2])
            for i in range(2):
                to_next[k, j, i] = forward[i]
                to_prev[k, j, i] = backward[i]

        @pl.when(early_next)
        def _():
            edge_forward(k).start()

        @pl.when(early_prev)
        def _():
            edge_backward(k).start()

        return 0

    lax.fori_loop(0, WINDOWS, edge_stage, 0)

    def middle_row(k, j):
        rows = rows_of(k, j)
        return row_lift(rows[0::2], rows[1::2], *[nothing] * 4)[1][1]

    def middle_stage(pair, _):
        k = 2 * pair
        a = [middle_row(k, j) for j in range(WIDE)]
        b = [middle_row(k + 1, j) for j in range(WIDE)]
        even, odd = split_pair(a, b, 1, lane_even)
        even, odd = column_lift(even, odd, 2, lane, KAPPA * KAPPA)
        for n, row in enumerate(join_pair(even, odd, 1, lane_even)):
            put_row(k + n, 3, row, first=True)
            start_blocks(k + n, 0)
        return 0

    lax.fori_loop(0, WINDOWS // 2, middle_stage, 0)

    @pl.when(late_next)
    def _():
        pl.semaphore_wait(ready.at[0], 1)

        def forward_stage(k, _):
            edge_forward(k).start()
            return 0

        lax.fori_loop(0, WINDOWS, forward_stage, 0)

    @pl.when(late_prev)
    def _():
        pl.semaphore_wait(ready.at[1], 1)

        def backward_stage(k, _):
            edge_backward(k).start()
            return 0

        lax.fori_loop(0, WINDOWS, backward_stage, 0)

    def wait_prev(k):
        @pl.when(has_prev)
        def _():
            edge_forward(k).wait_recv()

    def wait_next(k):
        @pl.when(has_next)
        def _():
            edge_backward(k).wait_recv()

    def row_1_stage(k):
        row_1 = []
        for j in range(WIDE):
            rows = rows_of(k, j)
            rest = [nothing] * 3
            row_1.append(row_lift(rows[0::2], rows[1::2], from_prev[k, j, 0], *rest)[1][0])
        even, odd = row_1, [turn(v, -1) for v in row_1]
        even, odd = column_lift(even, odd, 2, lane, KAPPA * KAPPA)
        put_row(k, 1, [jnp.where(lane_even, e, turn(o, 1)) for e, o in zip(even, odd)])
        start_blocks(k, 2)

    def rows_5_7_stage(k):
        row_5, row_7 = [], []
        for j in range(WIDE):
            rows = rows_of(k, j)
            edges = (nothing, nothing, from_next[k, j, 0], from_next[k, j, 1])
            odd = row_lift(rows[0::2], rows[1::2], *edges)[1]
            row_5.append(odd[2])
            row_7.append(odd[3])
        even, odd = split_pair(row_5, row_7, 1, lane_even)
        even, odd = column_lift(even, odd, 2, lane, KAPPA * KAPPA)
        row_5, row_7 = join_pair(even, odd, 1, lane_even)
        put_row(k, 5, row_5)
        put_row(k, 7, row_7)
        start_blocks(k, 1)

    def first_stage(k):
        w = window_of(k)
        for j in range(WIDE):
            rows = rows_of(k, j)
            even, _ = row_lift(
                rows[0::2],
                rows[1::2],
                from_prev[k, j, 0],
                from_prev[k, j, 1],
                from_next[k, j, 0],
                from_next[k, j, 1],
            )
            for i in range(4):
                window[i, j] = even[i]

        def split(a, b):
            tiles = [[window[i, j] for j in range(WIDE)] for i in (a, b)]
            return split_pair(*tiles, 1, lane_even)

        within = jnp.logical_or(
            lane < LAST,
            jnp.logical_or(
                jnp.logical_and(lane < LAST + HALO, w < WINDOWS - 1),
                jnp.logical_and(lane >= LAST + HALO, w > 0),
            ),
        )
        low_a, high_a = column_lift(*split(0, 2), 2, lane)
        low_b, high_b = column_lift(*split(1, 3), 2, lane)
        low_a[-1] = jnp.where(within, low_a[-1], 0.0)
        low_b[-1] = jnp.where(within, low_b[-1], 0.0)
        even, odd = split_pair(low_a, low_b, 2, lane_low)
        even, odd = column_lift(even, odd, 4, lane)
        low_a, low_b = join_pair(even, odd, 2, lane_low)
        c0, c2 = join_pair(low_a, high_a, 1, lane_even)
        c1, c3 = join_pair(low_b, high_b, 1, lane_even)
        for j in range(WIDE):
            for i, row in enumerate((c0, c1, c2, c3)):
                hold[k, i, j] = row[j]
            (p, q), (r, s) = row_messages([c0[j], c2[j]], [c1[j], c3[j]])
            to_next2[k, j] = jnp.where(lane_even, p, turn(q, 1))
            to_prev2[k, j] = jnp.where(lane_even, r, turn(s, 1))

        @pl.when(has_next)
        def _():
            edge2_forward(k).start()

        @pl.when(has_prev)
        def _():
            edge2_backward(k).start()

    square = KAPPA * KAPPA
    one = jnp.ones((ROWS, LANES), jnp.float32)
    scale_even = jnp.where(
        lane_even, jnp.where(lane_low, 1.0 / (square * square), 1.0 / square), one
    )
    scale_odd = jnp.where(jnp.logical_and(lane_even, lane_low), 1.0 / square, one)

    def second_stage(k):
        @pl.when(has_prev)
        def _():
            edge2_forward(k).wait_recv()

        @pl.when(has_next)
        def _():
            edge2_backward(k).wait_recv()

        rows = [[None] * WIDE for _ in range(4)]
        for j in range(WIDE):
            c = [hold[k, i, j] for i in range(4)]
            p = from_prev2[k, j]
            r = from_next2[k, j]
            even, odd = row_lift(c[0::2], c[1::2], p, turn(p, -1), r, turn(r, -1))
            for i in range(2):
                rows[2 * i][j] = jnp.where(lane_even, even[i], c[2 * i]) * scale_even
                rows[2 * i + 1][j] = jnp.where(lane_even, odd[i], c[2 * i + 1]) * scale_odd
        for i in range(4):
            put_row(k, 2 * i, rows[i], first=i == 0)
        start_blocks(k, 3)

    @pl.when(row_1_first)
    def _():
        def early_stage(k, _):
            wait_prev(k)
            row_1_stage(k)
            return 0

        lax.fori_loop(0, WINDOWS, early_stage, 0)

    @pl.when(seam_prev)
    def _():
        def early_stage(k, _):
            wait_next(k)
            rows_5_7_stage(k)
            return 0

        lax.fori_loop(0, WINDOWS, early_stage, 0)

    def stages(k, _):
        @pl.when(k < WINDOWS)
        def _():
            @pl.when(jnp.logical_not(row_1_first))
            def _():
                wait_prev(k)

            @pl.when(jnp.logical_not(seam_prev))
            def _():
                wait_next(k)

            first_stage(k)

            @pl.when(jnp.logical_not(row_1_first))
            def _():
                row_1_stage(k)

            @pl.when(jnp.logical_not(seam_prev))
            def _():
                rows_5_7_stage(k)

        @pl.when(k >= 2)
        def _():
            second_stage(k - 2)

        return 0

    lax.fori_loop(0, WINDOWS + 2, stages, 0)

    def spread(source):
        for row in range(ROWS):
            start = (source * ROWS + row) * SPAN * ROWS
            for j in range(FULL):
                levels[pl.ds(pl.multiple_of(start + j * ROWS, ROWS), ROWS), :] = recv[
                    source, pl.ds(ROW_AT[row] + j * ROWS, ROWS), :
                ]
            tail = recv[source, pl.ds(ODD_TAILS if row % 2 else EVEN_TAILS, ROWS), :]
            levels[pl.ds(pl.multiple_of(start + FULL * ROWS, ROWS), ROWS), :] = turn(
                tail, -TAIL * TAIL_AT[row]
            )

    low_taps, high_taps = tap_values()
    cutoffs = [cutoff_pattern(pointer_ref, part) for part in range(2)]

    def level_tile(source, level, j):
        start = source * ROWS * SPAN * ROWS + j * ROWS + level
        return levels[pl.ds(start, ROWS, stride=SPAN * ROWS), :]

    def put_pair(source, i, j, taken):
        for part, taps in enumerate((low_taps, high_taps)):
            value = taps[0] * taken[0]
            for tap in range(1, 4):
                value = value + taps[tap] * taken[tap]
            cutoff = cutoffs[part]
            value = value - jnp.minimum(jnp.maximum(value, -cutoff), cutoff)
            row = part * PARTS * ROWS // 2 + source * (ROWS // 2) + i
            if j == FULL:
                out_ref[row, :, pl.ds(FULL * LANES, TAIL)] = value[:, :TAIL]
            else:
                out_ref[row, :, pl.ds(j * LANES, LANES)] = value

    def store(source, part, last):
        start = part * PARTS * ROWS // 2 + source * (ROWS // 2)
        some = pl.ds(start + 3, 1) if last else pl.ds(start, 3)
        return pltpu.make_async_copy(
            out_ref.at[some], out_hbm.at[some], store_sem.at[2 * part + last, source]
        )

    def within_source(source):
        spread(source)
        for j in range(SPAN):
            taken = [level_tile(source, level, j) for level in range(ROWS)]
            for i in range(ROWS // 2 - 1):
                put_pair(source, i, j, taken[2 * i : 2 * i + 4])
        for part in range(2):
            store(source, part, 0).start()

    def arrived(n, _):
        step = (n + 1) // 2
        source = 2 * lax.rem(place + WINDOWS - step, WINDOWS) + lax.rem(half + n, 2)

        @pl.when(n == 0)
        def _():
            for piece in range(len(PIECES)):
                own_copy(piece).wait()

        @pl.when(n > 0)
        def _():
            for piece in range(len(PIECES)):
                from_source(source, piece).wait_recv()

        within_source(source)
        return 0

    lax.fori_loop(0, PARTS, arrived, 0)

    def across_sources(source, _):
        after = lax.rem(source + 1, PARTS)
        for j in range(SPAN):
            taken = [level_tile(source, level, j) for level in (ROWS - 2, ROWS - 1)]
            taken += [level_tile(after, level, j) for level in range(2)]
            put_pair(source, ROWS // 2 - 1, j, taken)
        for part in range(2):
            store(source, part, 1).start()
        return 0

    lax.fori_loop(0, PARTS, across_sources, 0)

    def sent(k, _):
        @pl.when(has_next)
        def _():
            edge_forward(k).wait_send()
            edge2_forward(k).wait_send()

        @pl.when(has_prev)
        def _():
            edge_backward(k).wait_send()
            edge2_backward(k).wait_send()

        for b in range(2):

            @pl.when(jnp.logical_not(jnp.logical_and(k == WINDOWS - 1, half == b)))
            def _():
                for piece in range(len(PIECES)):
                    block_copy(k, b, piece).wait_send()

        return 0

    lax.fori_loop(0, WINDOWS, sent, 0)

    def stored(source, _):
        for part in range(2):
            for last in range(2):
                store(source, part, last).wait()
        return 0

    lax.fori_loop(0, PARTS, stored, 0)


def local(tiles_count, thermal_deviation, terrain_flag, frequency_share_limit_pointer):
    tile = (ROWS, LANES)
    vmem = lambda *shape: pltpu.VMEM(shape, jnp.float32)
    dma = pltpu.SemaphoreType.DMA
    return pl.pallas_call(
        functools.partial(kernel, tiles_count),
        out_shape=jax.ShapeDtypeStruct((PARTS * ROWS, ROWS, BLOCK), jnp.float32),
        in_specs=[
            pl.BlockSpec(memory_space=pltpu.HBM),
            pl.BlockSpec(memory_space=pltpu.HBM),
            pl.BlockSpec(memory_space=pltpu.SMEM),
        ],
        out_specs=pl.BlockSpec(memory_space=pltpu.HBM),
        scratch_shapes=[
            vmem(PARTS * ROWS, ROWS, BLOCK),
            vmem(ROWS, ROWS, WIDTH),
            pltpu.VMEM((ROWS, WIDTH), jnp.int32),
            vmem(PADDED * GROUP, LANES),
            vmem(WINDOWS * WIDE * GROUP, LANES),
            vmem(WINDOWS, WIDE, 2, *tile),
            vmem(WINDOWS, WIDE, 2, *tile),
            vmem(WINDOWS, WIDE, 2, *tile),
            vmem(WINDOWS, WIDE, 2, *tile),
            vmem(4, WIDE, *tile),
            vmem(WINDOWS, 4, WIDE, *tile),
            vmem(WINDOWS, WIDE, *tile),
            vmem(WINDOWS, WIDE, *tile),
            vmem(WINDOWS, WIDE, *tile),
            vmem(WINDOWS, WIDE, *tile),
            vmem(PARTS, MESSAGE, LANES),
            vmem(PARTS, MESSAGE, LANES),
            vmem(PARTS * ROWS * SPAN * ROWS, LANES),
            dma((ROWS + 1,)),
            dma((2, WINDOWS)),
            dma((2, WINDOWS)),
            dma((2, WINDOWS)),
            dma((2, WINDOWS)),
            dma((len(PIECES), PARTS)),
            dma((len(PIECES), PARTS)),
            dma((len(PIECES),)),
            dma((4, PARTS)),
            pltpu.SemaphoreType.REGULAR((2,)),
        ],
        compiler_params=pltpu.CompilerParams(
            collective_id=0, has_side_effects=True, vmem_limit_bytes=60 * 1024 * 1024
        ),
    )(thermal_deviation, terrain_flag, frequency_share_limit_pointer)


def solution(mesh):
    placed = (P("lev", "tile", None), P("tile", None), P())
    return jax.shard_map(
        functools.partial(local, mesh.shape["tile"]),
        mesh=mesh,
        in_specs=placed,
        out_specs=P(None, "tile", "lev"),
        check_vma=False,
    )
```

time: 46.8 us -> 39.8 us (0.85)
  the two profiles are of different devices: /device:TPU:81 before, /device:TPU:40 now
where the time goes in v1:
time: 39.8 us; the launch traced here: 39.6 us
  Pallas kernels  37.2 us (93%)
  local copies, waits for them, and re-layouts  2.46 us (6%)
    pallas_call x1, Pallas kernels, local(): pl.pallas_call(functools.partial(kernel, tiles_count), out_shape=jax.Shap...  37.2 us
    unnamed x1, local copies, waits for them, and re-layouts  2.46 us

profile of v1, /device:TPU:40, one launch (start us, length us, event | category | flops | bytes accessed | tf_op | source)
XLA Modules:
  0.0 39.6 jit_solution(17142329202814421719)
XLA Ops:
  0.0 37.2 %shard_map.37 = f32[64,8,540]{2,1,0:T(8,128)} custom-call(f32[8,8,4320]{2,1,0:T(8,128)} %x_hbm.1, s32[8,4320]{1,0:T(8,128)} %flag_hbm.1, s32[14]{0:T(128)} %pointer_ref.1), custom_call_target="tpu_custom_call" | custom-call | tf_op jit(solution)/shard_map/pallas_call | solution.py:762
  37.2 2.5 %copy.5 = f32[64,8,540]{2,1,0:T(8,128)} copy(f32[64,8,540]{2,1,0:T(8,128)} %shard_map.37) | data formatting | bytes 2211840

commit v2 on v1

--- a/solution.py
+++ b/solution.py
@@ -158,9 +158,9 @@
     tiles_count,
     x_hbm,
     flag_hbm,
+    pointer_hbm,
+    out_ref,
     pointer_ref,
-    out_hbm,
-    out_ref,
     x_ref,
     flag_ref,
     field,
@@ -186,7 +186,6 @@
     block_send,
     block_recv,
     own_sem,
-    store_sem,
     ready,
 ):
     me = lax.axis_index("lev")
@@ -195,11 +194,12 @@
     has_prev = row_block > 0
     has_next = row_block < tiles_count - 1
     seam_prev = lax.rem(row_block, CHAIN) == 0
-    seam_next = lax.rem(row_block, CHAIN) == CHAIN - 1
-    early_prev = jnp.logical_and(has_prev, jnp.logical_not(seam_prev))
     late_prev = jnp.logical_and(has_prev, seam_prev)
-    early_next = jnp.logical_and(has_next, seam_next)
-    late_next = jnp.logical_and(has_next, jnp.logical_not(seam_next))
+    late_next = jnp.logical_and(has_next, lax.rem(row_block, CHAIN) == CHAIN // 2 - 1)
+    seen_by_prev = jnp.logical_and(has_prev, lax.rem(row_block, CHAIN) == CHAIN // 2)
+    seen_by_next = jnp.logical_and(has_next, lax.rem(row_block, CHAIN) == CHAIN - 1)
+    early_prev = jnp.logical_and(has_prev, jnp.logical_not(late_prev))
+    early_next = jnp.logical_and(has_next, jnp.logical_not(late_next))
     row_1_first = lax.rem(row_block, CHAIN) == 1
     lane = lax.broadcasted_iota(jnp.int32, (ROWS, LANES), 1)
     lane_even = lane % 2 == 0
@@ -215,13 +215,13 @@
             device_id_type=MESH,
         )
 
-    @pl.when(late_prev)
+    @pl.when(jnp.logical_and(has_prev, jnp.logical_not(seen_by_prev)))
     def _():
         pl.semaphore_signal(
             barrier, inc=1, device_id={"tile": row_block - 1}, device_id_type=MESH
         )
 
-    @pl.when(late_next)
+    @pl.when(jnp.logical_and(has_next, jnp.logical_not(seen_by_next)))
     def _():
         pl.semaphore_signal(
             barrier, inc=1, device_id={"tile": row_block + 1}, device_id_type=MESH
@@ -232,6 +232,7 @@
         for level in range(ROWS)
     ]
     loads.append(pltpu.make_async_copy(flag_hbm, flag_ref, load_sem.at[ROWS]))
+    loads.append(pltpu.make_async_copy(pointer_hbm, pointer_ref, load_sem.at[ROWS + 1]))
     for load in loads:
         load.start()
 
@@ -259,13 +260,13 @@
         barrier, PARTS - 1 + jnp.where(early_prev, 1, 0) + jnp.where(early_next, 1, 0)
     )
 
-    @pl.when(early_prev)
+    @pl.when(seen_by_prev)
     def _():
         pl.semaphore_signal(
             ready.at[0], inc=1, device_id={"tile": row_block - 1}, device_id_type=MESH
         )
 
-    @pl.when(early_next)
+    @pl.when(seen_by_next)
     def _():
         pl.semaphore_signal(
             ready.at[1], inc=1, device_id={"tile": row_block + 1}, device_id_type=MESH
@@ -473,16 +474,6 @@
 
         lax.fori_loop(0, WINDOWS, forward_stage, 0)
 
-    @pl.when(late_prev)
-    def _():
-        pl.semaphore_wait(ready.at[1], 1)
-
-        def backward_stage(k, _):
-            edge_backward(k).start()
-            return 0
-
-        lax.fori_loop(0, WINDOWS, backward_stage, 0)
-
     def wait_prev(k):
         @pl.when(has_prev)
         def _():
@@ -616,6 +607,16 @@
 
         lax.fori_loop(0, WINDOWS, early_stage, 0)
 
+    @pl.when(late_prev)
+    def _():
+        pl.semaphore_wait(ready.at[1], 1)
+
+        def backward_stage(k, _):
+            edge_backward(k).start()
+            return 0
+
+        lax.fori_loop(0, WINDOWS, backward_stage, 0)
+
     def stages(k, _):
         @pl.when(k < WINDOWS)
         def _():
@@ -677,21 +678,12 @@
             else:
                 out_ref[row, :, pl.ds(j * LANES, LANES)] = value
 
-    def store(source, part, last):
-        start = part * PARTS * ROWS // 2 + source * (ROWS // 2)
-        some = pl.ds(start + 3, 1) if last else pl.ds(start, 3)
-        return pltpu.make_async_copy(
-            out_ref.at[some], out_hbm.at[some], store_sem.at[2 * part + last, source]
-        )
-
     def within_source(source):
         spread(source)
         for j in range(SPAN):
             taken = [level_tile(source, level, j) for level in range(ROWS)]
             for i in range(ROWS // 2 - 1):
                 put_pair(source, i, j, taken[2 * i : 2 * i + 4])
-        for part in range(2):
-            store(source, part, 0).start()
 
     def arrived(n, _):
         step = (n + 1) // 2
@@ -718,8 +710,6 @@
             taken = [level_tile(source, level, j) for level in (ROWS - 2, ROWS - 1)]
             taken += [level_tile(after, level, j) for level in range(2)]
             put_pair(source, ROWS // 2 - 1, j, taken)
-        for part in range(2):
-            store(source, part, 1).start()
         return 0
 
     lax.fori_loop(0, PARTS, across_sources, 0)
@@ -745,14 +735,6 @@
         return 0
 
     lax.fori_loop(0, WINDOWS, sent, 0)
-
-    def stored(source, _):
-        for part in range(2):
-            for last in range(2):
-                store(source, part, last).wait()
-        return 0
-
-    lax.fori_loop(0, PARTS, stored, 0)
 
 
 def local(tiles_count, thermal_deviation, terrain_flag, frequency_share_limit_pointer):
@@ -761,15 +743,15 @@
     dma = pltpu.SemaphoreType.DMA
     return pl.pallas_call(
         functools.partial(kernel, tiles_count),
-        out_shape=jax.ShapeDtypeStruct((PARTS * ROWS, ROWS, BLOCK), jnp.float32),
+        out_shape=pltpu.VMEM((PARTS * ROWS, ROWS, BLOCK), jnp.float32),
         in_specs=[
             pl.BlockSpec(memory_space=pltpu.HBM),
             pl.BlockSpec(memory_space=pltpu.HBM),
-            pl.BlockSpec(memory_space=pltpu.SMEM),
+            pl.BlockSpec(memory_space=pltpu.HBM),
         ],
-        out_specs=pl.BlockSpec(memory_space=pltpu.HBM),
+        out_specs=pl.BlockSpec(memory_space=pltpu.VMEM),
         scratch_shapes=[
-            vmem(PARTS * ROWS, ROWS, BLOCK),
+            pltpu.SMEM((14,), jnp.int32),
             vmem(ROWS, ROWS, WIDTH),
             pltpu.VMEM((ROWS, WIDTH), jnp.int32),
             vmem(PADDED * GROUP, LANES),
@@ -787,7 +769,7 @@
             vmem(PARTS, MESSAGE, LANES),
             vmem(PARTS, MESSAGE, LANES),
             vmem(PARTS * ROWS * SPAN * ROWS, LANES),
-            dma((ROWS + 1,)),
+            dma((ROWS + 2,)),
             dma((2, WINDOWS)),
             dma((2, WINDOWS)),
             dma((2, WINDOWS)),
@@ -795,13 +777,16 @@
             dma((len(PIECES), PARTS)),
             dma((len(PIECES), PARTS)),
             dma((len(PIECES),)),
-            dma((4, PARTS)),
             pltpu.SemaphoreType.REGULAR((2,)),
         ],
         compiler_params=pltpu.CompilerParams(
-            collective_id=0, has_side_effects=True, vmem_limit_bytes=60 * 1024 * 1024
+            collective_id=0, has_side_effects=True, vmem_limit_bytes=40 * 1024 * 1024
         ),
-    )(thermal_deviation, terrain_flag, frequency_share_limit_pointer)
+    )(
+        pltpu.with_memory_space_constraint(thermal_deviation, pltpu.HBM),
+        pltpu.with_memory_space_constraint(terrain_flag, pltpu.HBM),
+        pltpu.with_memory_space_constraint(frequency_share_limit_pointer, pltpu.HBM),
+    )
 
 
 def solution(mesh):

time: 39.8 us -> 36.2 us (0.910)
  the two profiles are of different devices: /device:TPU:40 before, /device:TPU:1 now
where the time goes in v2:
time: 36.2 us; the launch traced here: 36 us
  Pallas kernels  34.9 us (96%)
  local copies, waits for them, and re-layouts  1.06 us (3%)
    pallas_call x1, Pallas kernels, local(): pl.pallas_call(functools.partial(kernel, tiles_count), out_shape=pltpu.VM...  34.9 us
    unnamed x1, local copies, waits for them, and re-layouts  1.06 us

profile of v2, /device:TPU:1, one launch (start us, length us, event | category | flops | bytes accessed | tf_op | source)
XLA Modules:
  0.0 36.0 jit_solution(11089778483512713500)
XLA Ops:
  0.0 34.9 %shard_map.37 = f32[64,8,540]{2,1,0:T(8,128)S(1)} custom-call(f32[8,8,4320]{2,1,0:T(8,128)} %x_hbm.1, s32[8,4320]{1,0:T(8,128)} %flag_hbm.1, s32[14]{0:T(128)} %pointer_hbm.1), custom_call_target="tpu_custom_call" | custom-call | tf_op jit(solution)/shard_map/pallas_call | solution.py:744
  34.9 1.1 %copy.5 = f32[64,8,540]{2,1,0:T(8,128)} copy(f32[64,8,540]{2,1,0:T(8,128)S(1)} %shard_map.37) | data formatting | bytes 2211840

commit v3 on v2

--- a/solution.py
+++ b/solution.py
@@ -195,11 +195,8 @@
     has_next = row_block < tiles_count - 1
     seam_prev = lax.rem(row_block, CHAIN) == 0
     late_prev = jnp.logical_and(has_prev, seam_prev)
-    late_next = jnp.logical_and(has_next, lax.rem(row_block, CHAIN) == CHAIN // 2 - 1)
-    seen_by_prev = jnp.logical_and(has_prev, lax.rem(row_block, CHAIN) == CHAIN // 2)
+    early_prev = jnp.logical_and(has_prev, jnp.logical_not(seam_prev))
     seen_by_next = jnp.logical_and(has_next, lax.rem(row_block, CHAIN) == CHAIN - 1)
-    early_prev = jnp.logical_and(has_prev, jnp.logical_not(late_prev))
-    early_next = jnp.logical_and(has_next, jnp.logical_not(late_next))
     row_1_first = lax.rem(row_block, CHAIN) == 1
     lane = lax.broadcasted_iota(jnp.int32, (ROWS, LANES), 1)
     lane_even = lane % 2 == 0
@@ -215,7 +212,7 @@
             device_id_type=MESH,
         )
 
-    @pl.when(jnp.logical_and(has_prev, jnp.logical_not(seen_by_prev)))
+    @pl.when(has_prev)
     def _():
         pl.semaphore_signal(
             barrier, inc=1, device_id={"tile": row_block - 1}, device_id_type=MESH
@@ -257,19 +254,13 @@
     field[pl.ds(0, GROUP), :] = jnp.zeros((GROUP, LANES), jnp.float32)
     field[pl.ds((PADDED - 2) * GROUP, 2 * GROUP), :] = jnp.zeros((2 * GROUP, LANES), jnp.float32)
     pl.semaphore_wait(
-        barrier, PARTS - 1 + jnp.where(early_prev, 1, 0) + jnp.where(early_next, 1, 0)
+        barrier, PARTS - 1 + jnp.where(early_prev, 1, 0) + jnp.where(has_next, 1, 0)
     )
-
-    @pl.when(seen_by_prev)
-    def _():
-        pl.semaphore_signal(
-            ready.at[0], inc=1, device_id={"tile": row_block - 1}, device_id_type=MESH
-        )
 
     @pl.when(seen_by_next)
     def _():
         pl.semaphore_signal(
-            ready.at[1], inc=1, device_id={"tile": row_block + 1}, device_id_type=MESH
+            ready, inc=1, device_id={"tile": row_block + 1}, device_id_type=MESH
         )
 
     for load in loads:
@@ -435,7 +426,7 @@
                 to_next[k, j, i] = forward[i]
                 to_prev[k, j, i] = backward[i]
 
-        @pl.when(early_next)
+        @pl.when(has_next)
         def _():
             edge_forward(k).start()
 
@@ -463,16 +454,6 @@
         return 0
 
     lax.fori_loop(0, WINDOWS // 2, middle_stage, 0)
-
-    @pl.when(late_next)
-    def _():
-        pl.semaphore_wait(ready.at[0], 1)
-
-        def forward_stage(k, _):
-            edge_forward(k).start()
-            return 0
-
-        lax.fori_loop(0, WINDOWS, forward_stage, 0)
 
     def wait_prev(k):
         @pl.when(has_prev)
@@ -609,7 +590,7 @@
 
     @pl.when(late_prev)
     def _():
-        pl.semaphore_wait(ready.at[1], 1)
+        pl.semaphore_wait(ready, 1)
 
         def backward_stage(k, _):
             edge_backward(k).start()
@@ -638,13 +619,13 @@
             def _():
                 rows_5_7_stage(k)
 
-        @pl.when(k >= 2)
-        def _():
-            second_stage(k - 2)
+        @pl.when(k >= 4)
+        def _():
+            second_stage(k - 4)
 
         return 0
 
-    lax.fori_loop(0, WINDOWS + 2, stages, 0)
+    lax.fori_loop(0, WINDOWS + 4, stages, 0)
 
     def spread(source):
         for row in range(ROWS):
@@ -777,7 +758,7 @@
             dma((len(PIECES), PARTS)),
             dma((len(PIECES), PARTS)),
             dma((len(PIECES),)),
-            pltpu.SemaphoreType.REGULAR((2,)),
+            pltpu.SemaphoreType.REGULAR,
         ],
         compiler_params=pltpu.CompilerParams(
             collective_id=0, has_side_effects=True, vmem_limit_bytes=40 * 1024 * 1024

time: 36.2 us -> 35.8 us (0.989)
  no operation moved by 1% of the time
where the time goes in v3:
time: 35.8 us; the launch traced here: 35.6 us
  Pallas kernels  34.6 us (97%)
  local copies, waits for them, and re-layouts  1.06 us (3%)
    pallas_call x1, Pallas kernels, local(): pl.pallas_call(functools.partial(kernel, tiles_count), out_shape=pltpu.VM...  34.6 us
    unnamed x1, local copies, waits for them, and re-layouts  1.06 us

profile of v3, /device:TPU:1, one launch (start us, length us, event | category | flops | bytes accessed | tf_op | source)
XLA Modules:
  0.0 35.6 jit_solution(3231648973933328023)
XLA Ops:
  0.0 34.6 %shard_map.37 = f32[64,8,540]{2,1,0:T(8,128)S(1)} custom-call(f32[8,8,4320]{2,1,0:T(8,128)} %x_hbm.1, s32[8,4320]{1,0:T(8,128)} %flag_hbm.1, s32[14]{0:T(128)} %pointer_hbm.1), custom_call_target="tpu_custom_call" | custom-call | tf_op jit(solution)/shard_map/pallas_call | solution.py:725
  34.6 1.1 %copy.5 = f32[64,8,540]{2,1,0:T(8,128)} copy(f32[64,8,540]{2,1,0:T(8,128)S(1)} %shard_map.37) | data formatting | bytes 2211840

commit v4 on v3

--- a/solution.py
+++ b/solution.py
@@ -736,7 +736,7 @@
             vmem(ROWS, ROWS, WIDTH),
             pltpu.VMEM((ROWS, WIDTH), jnp.int32),
             vmem(PADDED * GROUP, LANES),
-            vmem(WINDOWS * WIDE * GROUP, LANES),
+            vmem(WINDOWS * WIDE * GROUP + ROWS, LANES),
             vmem(WINDOWS, WIDE, 2, *tile),
             vmem(WINDOWS, WIDE, 2, *tile),
             vmem(WINDOWS, WIDE, 2, *tile),
@@ -749,7 +749,7 @@
             vmem(WINDOWS, WIDE, *tile),
             vmem(PARTS, MESSAGE, LANES),
             vmem(PARTS, MESSAGE, LANES),
-            vmem(PARTS * ROWS * SPAN * ROWS, LANES),
+            vmem((PARTS * ROWS + 1) * SPAN * ROWS, LANES),
             dma((ROWS + 2,)),
             dma((2, WINDOWS)),
             dma((2, WINDOWS)),

time: 35.8 us -> 35.8 us (level)
  no operation moved by 1% of the time
where the time goes in v4:
time: 35.8 us; the launch traced here: 35.6 us
  Pallas kernels  34.6 us (97%)
  local copies, waits for them, and re-layouts  1.06 us (3%)
    pallas_call x1, Pallas kernels, local(): pl.pallas_call(functools.partial(kernel, tiles_count), out_shape=pltpu.VM...  34.6 us
    unnamed x1, local copies, waits for them, and re-layouts  1.06 us

profile of v4, /device:TPU:1, one launch (start us, length us, event | category | flops | bytes accessed | tf_op | source)
XLA Modules:
  0.0 35.6 jit_solution(17852038858254663198)
XLA Ops:
  0.0 34.6 %shard_map.37 = f32[64,8,540]{2,1,0:T(8,128)S(1)} custom-call(f32[8,8,4320]{2,1,0:T(8,128)} %x_hbm.1, s32[8,4320]{1,0:T(8,128)} %flag_hbm.1, s32[14]{0:T(128)} %pointer_hbm.1), custom_call_target="tpu_custom_call" | custom-call | tf_op jit(solution)/shard_map/pallas_call | solution.py:725
  34.6 1.1 %copy.5 = f32[64,8,540]{2,1,0:T(8,128)} copy(f32[64,8,540]{2,1,0:T(8,128)S(1)} %shard_map.37) | data formatting | bytes 2211840
